TPU v7x, 512 devices: a whole 4x4x16 slice. The times are simulated.
512 devices in a mesh: rep: 8 (over z_lo), fsdp: 64 (over y, x, z_hi, core).
Axes of the slice: x: 4, y: 4, z: 16 (z_hi: 2, z_lo: 8; z = z_hi * 8 + z_lo), core: 2. Of those that a mesh axis runs over, the one named last changes fastest.
Arguments:
- inputs: bfloat16 [8, 8192, 7168], P('rep', 'fsdp'), may hold values from -6 to 6
- cotangent: bfloat16 [8, 8192, 7168], P('rep', 'fsdp'), may hold values from -6 to 6
- weights: float32 [8, 2, 3584, 128], P('rep', None, 'fsdp'), may hold values from -6 to 6
- first_moment: float32 [8, 2, 3584, 128], P('rep', None, 'fsdp'), may hold values from -0.015625 to 0.015625
- second_moment: float32 [8, 2, 3584, 128], P('rep', None, 'fsdp'), may hold values from 1e-08 to 1e-05
- anchor: float32 [3584, 128], P('fsdp'), may hold values from -6 to 6
- momentum: float32 [3584, 128], P('fsdp'), may hold values from -4 to 4
- fragment: int32 [1], replicated, may hold values from 1 to 64
Outputs:
- new_weights: float32 [8, 2, 3584, 128], P('rep', None, 'fsdp')
- new_anchor: float32 [3584, 128], P('fsdp')
- new_momentum: float32 [3584, 128], P('fsdp')
All inputs are finite; a program needn't handle non-finite values.
Results may differ from a plain program's by a relative error of at most 0.0022.
Values may be sent and summed in bfloat16 or wider, within the bound.
A program may use at most 64 MiB of HBM per device.

v0:
```python
import math

import jax
import jax.numpy as jnp
from jax import lax
from jax.sharding import PartitionSpec as P

norm_eps = 1e-05
beta_one = 0.9
beta_two = 0.95
adam_eps = 1e-08
decay_rate = 0.1
inner_rate = 0.05
outer_rate = 0.7
outer_beta = 0.9
mixing = 0.5


def layer_forward(hidden_in, w_in, w_out):
    inputs_f32 = hidden_in.astype(jnp.float32)
    inv_rms = lax.rsqrt(jnp.mean(inputs_f32 * inputs_f32, axis=-1, keepdims=True) + norm_eps)
    normed = (inputs_f32 * inv_rms).astype(jnp.bfloat16)
    in_scale = w_in.shape[1] ** (-0.5)
    out_scale = w_out.shape[0] ** (-0.5)
    pre_act = (
        lax.dot_general(normed, w_in, (((1,), (1,)), ((), ())), preferred_element_type=jnp.float32)
        * in_scale
    )
    activated = jax.nn.silu(pre_act).astype(jnp.bfloat16)
    layer_out = (
        inputs_f32 + jnp.dot(activated, w_out, preferred_element_type=jnp.float32) * out_scale
    ).astype(jnp.bfloat16)
    return (layer_out, (inputs_f32, inv_rms, normed, pre_act, activated))


def layer_backward(grad_out, w_in, w_out, saved, need_input):
    inputs_f32, inv_rms, normed, pre_act, activated = saved
    in_scale = w_in.shape[1] ** (-0.5)
    out_scale = w_out.shape[0] ** (-0.5)
    grad_w_out = (
        lax.dot_general(
            activated, grad_out, (((0,), (0,)), ((), ())), preferred_element_type=jnp.float32
        )
        * out_scale
    )
    grad_act = (
        lax.dot_general(
            grad_out, w_out, (((1,), (1,)), ((), ())), preferred_element_type=jnp.float32
        )
        * out_scale
    )
    sigmoid_pre = jax.nn.sigmoid(pre_act)
    grad_pre = (grad_act * sigmoid_pre * (1.0 + pre_act * (1.0 - sigmoid_pre))).astype(jnp.bfloat16)
    grad_w_in = (
        lax.dot_general(
            grad_pre, normed, (((0,), (0,)), ((), ())), preferred_element_type=jnp.float32
        )
        * in_scale
    )
    if not need_input:
        return (grad_w_in, grad_w_out, grad_out)
    grad_norm = jnp.dot(grad_pre, w_in, preferred_element_type=jnp.float32) * in_scale
    inner_sum = jnp.sum(grad_norm * inputs_f32, axis=-1, keepdims=True) / inputs_f32.shape[1]
    grad_in = (
        grad_out.astype(jnp.float32)
        + inv_rms * grad_norm
        - inputs_f32 * (inv_rms * inv_rms * inv_rms) * inner_sum
    )
    return (grad_w_in, grad_w_out, grad_in.astype(jnp.bfloat16))


def outer_step(total, base, velocity, replicas):
    mean_delta = total / replicas
    new_velocity = outer_beta * velocity + mean_delta
    new_global = base - outer_rate * (mean_delta + outer_beta * new_velocity)
    return (new_global, new_velocity)


def shards(inputs, cotangent, weights, first_moment, second_moment, anchor, momentum, fragment):
    tokens = inputs[0]
    upstream = cotangent[0]
    params = weights[0]
    layers = params.shape[0]
    model_width = tokens.shape[1]
    groups = lax.axis_size("fsdp")
    flat_rows = params.shape[1] * groups
    hidden = flat_rows * 128 // (2 * model_width)
    compact = params.astype(jnp.bfloat16)
    gathered_all = lax.all_gather(compact, "fsdp", axis=1, tiled=True).reshape(
        layers, 2, hidden, model_width
    )
    pairs = []
    saved_list = []
    current = tokens
    for layer_index in range(layers):
        weight_pair = gathered_all[layer_index]
        pairs.append(weight_pair)
        current, saved = layer_forward(current, weight_pair[0], weight_pair[1])
        saved_list.append(saved)
    partials = [None] * layers
    for layer_index in reversed(range(layers)):
        weight_pair = pairs[layer_index]
        grad_w_in, grad_w_out, upstream = layer_backward(
            upstream, weight_pair[0], weight_pair[1], saved_list[layer_index], layer_index > 0
        )
        term = jnp.stack([grad_w_in, grad_w_out]).reshape(flat_rows, 128)
        partials[layer_index] = term
    summed = lax.psum_scatter(jnp.stack(partials), "fsdp", scatter_dimension=1, tiled=True)
    gradient = summed / (tokens.shape[0] * groups)
    count = fragment[0]
    chosen = jnp.remainder(count, layers)
    count_real = count.astype(jnp.float32)
    correct_one = 1.0 - jnp.exp(count_real * math.log(beta_one))
    correct_two = 1.0 - jnp.exp(count_real * math.log(beta_two))
    moment_one = beta_one * first_moment[0] + (1.0 - beta_one) * gradient
    moment_two = beta_two * second_moment[0] + (1.0 - beta_two) * gradient * gradient
    updated = params - inner_rate * (
        moment_one / correct_one / (jnp.sqrt(moment_two / correct_two) + adam_eps)
        + decay_rate * params
    )
    pseudo = anchor - lax.dynamic_index_in_dim(params, chosen, 0, keepdims=False)
    replicas = lax.axis_size("rep")
    total = lax.psum(pseudo, "rep")
    new_global, new_velocity = outer_step(total, anchor, momentum, replicas)
    selector = (jnp.arange(layers, dtype=jnp.int32) == chosen)[:, None, None]
    merged = jnp.where(selector, mixing * updated + (1.0 - mixing) * new_global[None], updated)
    return (merged[None], new_global, new_velocity)


def solution(mesh):
    placed = (
        P("rep", "fsdp", None),
        P("rep", "fsdp", None),
        P("rep", None, "fsdp", None),
        P("rep", None, "fsdp", None),
        P("rep", None, "fsdp", None),
        P("fsdp", None),
        P("fsdp", None),
        P(),
    )
    return jax.shard_map(
        shards,
        mesh=mesh,
        in_specs=placed,
        out_specs=(P("rep", None, "fsdp", None), P("fsdp", None), P("fsdp", None)),
        check_vma=False,
    )
```

profile of v0, /device:TPU:1, one launch (start us, length us, event | category | flops | bytes accessed | tf_op | source)
XLA Modules:
  0.0 735.1 jit_solution(16683716544999077860)
XLA Ops:
  7.2 1.4 bitcast_convert_fusion
  8.7 1.9 fusion.9
  10.7 119.2 %all-gather.2.cloned.1.call-done = bf16[2,3584,128]{2,1,0:T(8,128)(2,1)} async-done(((bf16[2,56,128]{2,1,0:T(8,128)(2,1)}), bf16[2,3584,128]{2,1,0:T(8,128)(2,1)}) %all-gather.2.cloned.1.call-update) | async-done | bytes 1835024 | tf_op jit(solution)/shard_map/all_gather | solution.py:89
  129.9 2.3 fusion.54
  132.2 1.0 squeeze.36
  133.9 1.8 fusion.21
  135.7 2.7 multiply_reduce_fusion.1
  138.4 1.2 squeeze.38
  139.6 1.0 squeeze.35
  140.6 3.0 convolution_multiply_fusion.6
  143.6 2.2 fusion.36
  147.3 2.6 subtract_convert_fusion
  149.9 3.9 fusion.3
  153.8 1.9 fusion.4
  155.6 2.6 fusion.5
  158.3 1.3 fusion.6
  159.6 1.4 pad_maximum_fusion.1
  161.0 1.6 stack_reshape.6
  162.6 2.5 pad_maximum_fusion.2
  165.1 2.7 stack_reshape.7
  167.9 3.5 pad_maximum_fusion
  172.3 43.4 %psum.7 = f32[56,128]{1,0:T(8,128)S(1)} all-reduce(f32[56,128]{1,0:T(8,128)S(1)} %bitcast_subtract_fusion.1), channel_id=1, replica_groups=mesh['rep'=8,'fsdp'=64] {'rep'}, use_global_device_ids=true, to_apply=%region_4.5 | all-reduce | flops 7168 | bytes 57344 | tf_op jit(solution)/shard_map/psum | solution.py:123
  216.4 510.4 %reduce-scatter.2.cloned.1.call-done = f32[2,56,128]{2,1,0:T(8,128)} async-done(((f32[2,3584,128]{2,1,0:T(8,128)}), f32[2,56,128]{2,1,0:T(8,128)}) %reduce-scatter.2.cloned.1.call-update) | async-done | bytes 57360 | tf_op jit(solution)/shard_map/reduce_scatter | solution.py:108
  726.8 1.5 select_bitcast_fusion
  (34 shorter events, 3.0 us)
Async XLA Ops:
  7.2 122.7 %all-gather.2.cloned.1.call-start = ((), (), s32[]{:S(2)}) async-start(), calls=%async_computation.1 | async-start | bytes 1863680 | tf_op jit(solution)/shard_map/all_gather | solution.py:89
  8.7 718.1 %reduce-scatter.2.cloned.1.call-start = ((), (), s32[]{:S(2)}) async-start(), calls=%async_computation.2 | async-start | bytes 3727360 | tf_op jit(solution)/shard_map/reduce_scatter | solution.py:108
  132.2 1.7 copy-start.1
  140.6 3.0 copy-start.5
  140.6 5.2 copy-start
  145.8 1.5 copy-start.2
  155.6 2.6 copy-start.3
  158.3 1.4 copy-start.4
  171.4 0.9 copy-start.6
  171.4 0.9 copy-start.7
  171.4 44.3 %copy-start.10 = (f32[56,128]{1,0:T(8,128)S(1)}, f32[56,128]{1,0:T(8,128)}, u32[]{:S(2)}) copy-start(f32[56,128]{1,0:T(8,128)} %param.14) | copy-start | bytes 86020
  171.4 555.4 %copy-start.8 = (f32[1,2,56,128]{3,2,1,0:T(8,128)S(1)}, f32[1,2,56,128]{3,2,1,0:T(8,128)}, u32[]{:S(2)}) copy-start(f32[1,2,56,128]{3,2,1,0:T(8,128)} %param.12) | copy-start | bytes 172036
  171.4 555.4 %copy-start.9 = (f32[1,2,56,128]{3,2,1,0:T(8,128)S(1)}, f32[1,2,56,128]{3,2,1,0:T(8,128)}, u32[]{:S(2)}) copy-start(f32[1,2,56,128]{3,2,1,0:T(8,128)} %param.11) | copy-start | bytes 172036
Sparse Core Ops, SparseCore 0:
  13.0 116.8 all-gather.1
  171.5 555.1 reduce-scatter.1
where the time goes:
time: 749 us; the launch traced here: 735 us
  waiting for transfers between devices  630 us (84%)
  blocking collectives  43.4 us (6%)
  matrix products  20.1 us (3%)
  other arithmetic  15.6 us (2%)
  between operations  15 us (2%)
  local copies, waits for them, and re-layouts  11.3 us (2%)
    reduce_scatter x1, waiting for transfers between devices, shards(): lax.psum_scatter(jnp.stack(partials), 'fsdp', scatter_dimension=1, tiled=...  510 us
    all_gather x1, waiting for transfers between devices, shards(): lax.all_gather(compact, 'fsdp', axis=1, tiled=True)  119 us
    psum x1, blocking collectives, shards(): total = lax.psum(pseudo, 'rep')  43.4 us
  transfers between devices with their start and end apart: 2, of which 2 were waited for; matrix products, arithmetic and copies ran while one was open for 0% of the time, Pallas kernels for 0%

commit v1 on v0

v1 whole, which is shorter than its diff:
```python
import math

import jax
import jax.numpy as jnp
from jax import lax
from jax.experimental import pallas as pl
from jax.experimental.pallas import tpu as pltpu
from jax.sharding import PartitionSpec as P

norm_eps = 1e-05
beta_one = 0.9
beta_two = 0.95
adam_eps = 1e-08
decay_rate = 0.1
inner_rate = 0.05
outer_rate = 0.7
outer_beta = 0.9
mixing = 0.5

MESH = pl.DeviceIdType.MESH
TOK = 128
D = 7168
H = 32
ROWS = 56
PLANE = 16
REPS = 8
F32 = jnp.float32
BF16 = jnp.bfloat16
CHIP = 2 * TOK
GRADS = CHIP
STACK = 2 * CHIP
ALL = STACK + 4 * H

NT = (((1,), (1,)), ((), ()))
NN = (((1,), (0,)), ((), ()))


def dot(a, b, dims):
    return lax.dot_general(a, b, dims, preferred_element_type=F32)


def kernel(
    x_h, g_h, w_h, fm_h, sm_h, an_h, mo_h, fr,
    new_w, new_a, new_m,
    stack, w_all, send, recv, z_send, z_recv, w_own, fm, sm, an, mo, rep_send, rep_recv,
    proj, coef, expand, flat, ss,
    load_sem, z_sems, ring_send, ring_recv, fwd_send, fwd_recv, tok_send, tok_recv,
    red_send, red_recv, rep_sems, rep_rsem,
):
    rep = lax.axis_index("rep")
    fsdp = lax.axis_index("fsdp")
    place = fsdp // 4
    zh = (fsdp // 2) % 2
    core = fsdp % 2

    def peer(k):
        return lax.rem(place + k, PLANE)

    def in_plane(q):
        return (rep, q * 4 + zh * 2 + core)

    other_z = (rep, place * 4 + (1 - zh) * 2 + core)
    sibling = (rep, place * 4 + zh * 2 + (1 - core))

    def rep_peer(k):
        return (lax.rem(rep + k, REPS), fsdp)

    def remote(src, dst, ssem, rsem, device):
        return pltpu.make_async_remote_copy(
            src_ref=src, dst_ref=dst, send_sem=ssem, recv_sem=rsem, device_id=device, device_id_type=MESH
        )

    barrier = pltpu.get_barrier_semaphore()

    def greet(device):
        pl.semaphore_signal(barrier, inc=1, device_id=device, device_id_type=MESH)

    greet(other_z)

    def greet_rep(k, _):
        greet(rep_peer(k))
        return 0

    lax.fori_loop(1, REPS, greet_rep, 0)
    greet(sibling)

    def greet_plane(k, _):
        greet(in_plane(peer(k)))
        return 0

    lax.fori_loop(1, PLANE, greet_plane, 0)

    loads = [
        pltpu.make_async_copy(src, dst, load_sem.at[i])
        for i, (src, dst) in enumerate(
            [
                (w_h.at[0], w_own),
                (x_h.at[0], stack.at[pl.ds(0, TOK)]),
                (g_h.at[0], stack.at[pl.ds(GRADS, TOK)]),
                (fm_h.at[0], fm),
                (sm_h.at[0], sm),
                (an_h, an),
                (mo_h, mo),
            ]
        )
    ]
    for load in loads:
        load.start()
    loads[0].wait()
    flat[pl.ds(0, ROWS, stride=2), :] = w_own[0]
    flat[pl.ds(1, ROWS, stride=2), :] = w_own[1]
    w_all[0, 0, place] = flat[...].astype(BF16).reshape(ROWS, 2, 128)
    step = fr[0]
    chosen = lax.rem(step, 2).astype(F32)
    rep_send[...] = w_own[0] * (1.0 - chosen) + w_own[1] * chosen

    pl.semaphore_wait(barrier, 1 + 1 + (PLANE - 1) + (REPS - 1))

    z_copy = remote(w_all.at[0, 0, place], w_all.at[1, 0, place], z_sems.at[0], z_sems.at[1], other_z)
    z_copy.start()

    def spread(h):
        def one(k, _):
            remote(
                w_all.at[h, 0, place], w_all.at[h, 0, place], ring_send.at[h], ring_recv.at[h, place], in_plane(peer(k))
            ).start()
            return 0

        lax.fori_loop(1, PLANE, one, 0)

    def hand_on(h, q):
        remote(w_all.at[h, 0, q], w_all.at[h, 1, q], fwd_send.at[h], fwd_recv.at[h], sibling).start()

    def collect(h):
        def one(k, _):
            q = lax.rem(place + PLANE - k, PLANE)
            remote(
                w_all.at[h, 0, q], w_all.at[h, 0, q], ring_send.at[h], ring_recv.at[h, q], in_plane(q)
            ).wait_recv()
            hand_on(h, q)
            return 0

        lax.fori_loop(1, PLANE, one, 0)

    spread(0)
    hand_on(0, place)
    tok_copies = []
    for i, start in enumerate((0, GRADS)):
        loads[1 + i].wait()
        copy = remote(
            stack.at[pl.ds(start, TOK)], stack.at[pl.ds(start + TOK, TOK)], tok_send.at[i], tok_recv.at[i], sibling
        )
        copy.start()
        tok_copies.append(copy)
    collect(0)
    z_copy.wait_recv()
    spread(1)
    hand_on(1, place)

    def rep_out(k, _):
        remote(rep_send, rep_recv.at[rep], rep_sems, rep_rsem.at[rep], rep_peer(k)).start()
        return 0

    lax.fori_loop(1, REPS, rep_out, 0)

    def relayout(h):
        remote(w_all.at[h, 0], w_all.at[h, 1], fwd_send.at[h], fwd_recv.at[h], sibling).wait_recv()

        def one(r, _):
            at = pl.multiple_of(r * 128, 128)
            for c in range(2):
                stack[pl.ds(STACK + h * 64 + c * 32, 32), pl.ds(at, 128)] = w_all[h, c, :, r].reshape(32, 128)
            return 0

        lax.fori_loop(0, ROWS, one, 0, unroll=4)

    relayout(0)
    for copy in tok_copies:
        copy.wait_recv()

    def square(r, acc):
        v = stack[pl.ds(0, CHIP), pl.ds(pl.multiple_of(r * 128, 128), 128)].astype(F32)
        return acc + v * v

    acc = lax.fori_loop(0, ROWS, square, jnp.zeros((CHIP, 128), F32))
    ss[...] = jnp.sum(acc.T, axis=0, keepdims=True)

    collect(1)
    relayout(1)

    proj[...] = jnp.zeros_like(proj)

    def project(i, _):
        at = pl.multiple_of(i * 1024, 1024)
        out = dot(stack[pl.ds(STACK, 4 * H), pl.ds(at, 1024)], stack[:, pl.ds(at, 1024)], NT)
        for j in range(ALL // 128):
            proj[j] += out[:, j * 128 : (j + 1) * 128]
        return 0

    lax.fori_loop(0, D // 1024, project, 0)

    def rows_of(kind, layer, cols):
        return jnp.concatenate(
            [
                jnp.concatenate([proj[j, pl.ds(hc * 32 + kind * 16 + layer, 8, stride=2), :] for hc in range(4)], axis=0)
                for j in cols
            ],
            axis=1,
        )

    tokens, grads, units = (0, 1), (2, 3), (4,)
    in_scale = D ** (-0.5)
    out_scale = H ** (-0.5)

    def put(kind, layer, v):
        expand[...] = jnp.zeros_like(expand)
        for j in range(2):
            for hc in range(4):
                expand[j, pl.ds(hc * 32 + kind * 16 + layer, 8, stride=2), :] = v[
                    hc * 8 : hc * 8 + 8, j * 128 : (j + 1) * 128
                ]
        return jnp.concatenate([expand[0], expand[1]], axis=1).astype(BF16)

    ss0 = ss[...]
    inv0 = lax.rsqrt(ss0 * (1.0 / D) + norm_eps)
    pre0 = rows_of(0, 0, tokens) * (inv0 * in_scale)
    sig0 = jax.nn.sigmoid(pre0)
    act0 = pre0 * sig0 * out_scale
    out0_h = rows_of(1, 0, tokens)
    gram = jnp.concatenate([rows_of(0, 1, units), rows_of(1, 0, units)], axis=0).astype(BF16)
    act_e = put(1, 0, act0)
    mixed = dot(gram, act_e, NN)
    in1_h1 = rows_of(0, 1, tokens) + mixed[0:H]
    out0_h1 = out0_h + mixed[H : 2 * H]
    ss1 = ss0 + jnp.sum(act0 * (out0_h + out0_h1), axis=0, keepdims=True)
    inv1 = lax.rsqrt(jnp.maximum(ss1, 0.0) * (1.0 / D) + norm_eps)
    pre1 = in1_h1 * (inv1 * in_scale)
    sig1 = jax.nn.sigmoid(pre1)
    act1 = pre1 * sig1 * out_scale
    grad_pre1 = rows_of(1, 1, grads) * out_scale * sig1 * (1.0 + pre1 * (1.0 - sig1))
    back = grad_pre1 * (inv1 * in_scale)
    pull = (inv1 * inv1 * (1.0 / D)) * jnp.sum(back * in1_h1, axis=0, keepdims=True)
    back_e = put(0, 1, back)
    grad_act0 = rows_of(1, 0, grads) + dot(gram[H : 2 * H], back_e, NN) - pull * out0_h1
    grad_pre0 = grad_act0 * out_scale * sig0 * (1.0 + pre0 * (1.0 - sig0))

    act0_b = act0.astype(BF16)
    pulled = act0 * pull
    mix1 = dot(back.astype(BF16), act_e, NT)
    mix0 = dot(act0_b, back_e, NT) - dot(pulled.astype(BF16), act_e, NT)
    zero = jnp.zeros((H, CHIP), F32)
    zero_u = jnp.zeros((H, 4 * H), F32)
    for kind, layer, parts in (
        (0, 0, (grad_pre0 * (inv0 * in_scale), zero, zero_u)),
        (0, 1, (back, zero, mix1)),
        (1, 0, (-pulled, act0, mix0)),
        (1, 1, (zero, act1, zero_u)),
    ):
        for h in range(2):
            for part, cols in zip(parts, (tokens, grads, units), strict=True):
                for i, j in enumerate(cols):
                    coef[j, pl.ds(h * 32 + kind * 16 + layer, 8, stride=2), :] = part[
                        h * 16 : h * 16 + 8, i * 128 : (i + 1) * 128
                    ]

    def gradients(h):
        weights = jnp.concatenate([coef[j, pl.ds(h * 32, 32), :] for j in range(ALL // 128)], axis=1).astype(BF16)

        def one(i, _):
            at = pl.multiple_of(i * 512, 512)
            out = dot(weights, stack[:, pl.ds(at, 512)], NN).astype(BF16)
            for j in range(4):
                send[h, :, i * 4 + j] = out[:, j * 128 : (j + 1) * 128].reshape(PLANE, 2, 128)
            return 0

        lax.fori_loop(0, D // 512, one, 0)

        def out_one(k, _):
            q = peer(k)
            remote(
                send.at[h, q], recv.at[h, place], red_send.at[h], red_recv.at[h], in_plane(q)
            ).start()
            return 0

        lax.fori_loop(1, PLANE, out_one, 0)
        recv[h, place] = send[h, place]

    def summed(h):
        pltpu.make_async_copy(
            recv.at[h, pl.ds(0, PLANE - 1)], recv.at[h, pl.ds(0, PLANE - 1)], red_recv.at[h]
        ).wait()
        total = recv[h, 0].reshape(2 * ROWS, 128).astype(F32)
        for q in range(1, PLANE):
            total += recv[h, q].reshape(2 * ROWS, 128).astype(F32)
        return total

    gradients(1)
    gradients(0)
    z_send[...] = summed(1).astype(BF16).reshape(ROWS, 2, 128)
    z_back = remote(z_send, z_recv, z_sems.at[2], z_sems.at[3], other_z)
    z_back.start()

    for load in loads[3:]:
        load.wait()

    def rep_in(k, _):
        q = lax.rem(rep + k, REPS)
        remote(rep_send, rep_recv.at[q], rep_sems, rep_rsem.at[q], rep_peer(k)).wait_recv()
        return 0

    lax.fori_loop(1, REPS, rep_in, 0)
    rep_recv[rep] = rep_send[...]
    anchor = an[...]
    total = anchor - rep_recv[0]
    for q in range(1, REPS):
        total += anchor - rep_recv[q]
    delta = total * (1.0 / REPS)
    velocity = outer_beta * mo[...] + delta
    new_anchor = anchor - outer_rate * (delta + outer_beta * velocity)
    new_m[...] = velocity
    new_a[...] = new_anchor

    own = summed(0)
    z_back.wait_recv()
    flat[...] = (own + z_recv[...].reshape(2 * ROWS, 128).astype(F32)) * (1.0 / (TOK * 64))
    count = jnp.full((8, 128), step.astype(F32), F32)
    correct_one = (1.0 - jnp.exp(count * math.log(beta_one)))[0:1]
    correct_two = (1.0 - jnp.exp(count * math.log(beta_two)))[0:1]
    for layer in range(2):
        gradient = flat[pl.ds(layer, ROWS, stride=2), :]
        params = w_own[layer]
        one = beta_one * fm[layer] + (1.0 - beta_one) * gradient
        two = beta_two * sm[layer] + (1.0 - beta_two) * gradient * gradient
        updated = params - inner_rate * (
            one / correct_one / (jnp.sqrt(two / correct_two) + adam_eps) + decay_rate * params
        )
        merged = mixing * updated + (1.0 - mixing) * new_anchor
        here = chosen if layer == 1 else 1.0 - chosen
        new_w[0, layer] = jnp.where(jnp.full((ROWS, 128), here, F32) > 0.5, merged, updated)

    z_copy.wait_send()
    z_back.wait_send()
    for copy in tok_copies:
        copy.wait_send()
    for h in range(2):
        most = w_all.at[h, 0, pl.ds(0, PLANE - 1)]
        pltpu.make_async_copy(most, most, ring_send.at[h]).wait()
        pltpu.make_async_copy(w_all.at[h, 0], w_all.at[h, 0], fwd_send.at[h]).wait()
        most = send.at[h, pl.ds(0, PLANE - 1)]
        pltpu.make_async_copy(most, most, red_send.at[h]).wait()
    most = rep_recv.at[pl.ds(0, REPS - 1)]
    pltpu.make_async_copy(most, most, rep_sems).wait()


def shards(inputs, cotangent, weights, first_moment, second_moment, anchor, momentum, fragment):
    any_space = pl.BlockSpec(memory_space=pl.ANY)
    vmem = pl.BlockSpec(memory_space=pltpu.VMEM)
    dma = pltpu.SemaphoreType.DMA
    unit = (ROWS, 2, 128)
    return pl.pallas_call(
        kernel,
        out_shape=(
            jax.ShapeDtypeStruct((1, 2, ROWS, 128), F32),
            jax.ShapeDtypeStruct((ROWS, 128), F32),
            jax.ShapeDtypeStruct((ROWS, 128), F32),
        ),
        in_specs=[any_space] * 7 + [pl.BlockSpec(memory_space=pltpu.SMEM)],
        out_specs=(vmem, vmem, vmem),
        scratch_shapes=[
            pltpu.VMEM((ALL, D), BF16),
            pltpu.VMEM((2, 2, PLANE) + unit, BF16),
            pltpu.VMEM((2, PLANE) + unit, BF16),
            pltpu.VMEM((2, PLANE) + unit, BF16),
            pltpu.VMEM(unit, BF16),
            pltpu.VMEM(unit, BF16),
            pltpu.VMEM((2, ROWS, 128), F32),
            pltpu.VMEM((2, ROWS, 128), F32),
            pltpu.VMEM((2, ROWS, 128), F32),
            pltpu.VMEM((ROWS, 128), F32),
            pltpu.VMEM((ROWS, 128), F32),
            pltpu.VMEM((ROWS, 128), F32),
            pltpu.VMEM((REPS, ROWS, 128), F32),
            pltpu.VMEM((ALL // 128, 4 * H, 128), F32),
            pltpu.VMEM((ALL // 128, 2 * H, 128), F32),
            pltpu.VMEM((2, 4 * H, 128), F32),
            pltpu.VMEM((2 * ROWS, 128), F32),
            pltpu.VMEM((1, CHIP), F32),
            dma((7,)),
            dma((4,)),
            dma((2,)),
            dma((2, PLANE)),
            dma((2,)),
            dma((2,)),
            dma((2,)),
            dma((2,)),
            dma((2,)),
            dma((2,)),
            dma,
            dma((REPS,)),
        ],
        compiler_params=pltpu.CompilerParams(
            collective_id=0, has_side_effects=True, vmem_limit_bytes=56 * 1024 * 1024
        ),
        name="window",
    )(inputs, cotangent, weights, first_moment, second_moment, anchor, momentum, fragment)


def solution(mesh):
    placed = (
        P("rep", "fsdp", None),
        P("rep", "fsdp", None),
        P("rep", None, "fsdp", None),
        P("rep", None, "fsdp", None),
        P("rep", None, "fsdp", None),
        P("fsdp", None),
        P("fsdp", None),
        P(),
    )
    return jax.shard_map(
        shards,
        mesh=mesh,
        in_specs=placed,
        out_specs=(P("rep", None, "fsdp", None), P("fsdp", None), P("fsdp", None)),
        check_vma=False,
    )
```

time: 749 us -> 67.3 us (0.09); the launches traced: 735 us -> 67 us
  waiting for transfers between devices: 630 us -> 0 us
  Pallas kernels: 0 us -> 61.5 us
  blocking collectives: 43.4 us -> 0 us
  matrix products: 20.1 us -> 0 us
  other arithmetic: 15.6 us -> 0 us
  between operations: 15 us -> 1.29 us
    reduce_scatter x1 -> x0, waiting for transfers between devices: 510 us -> none  [shards(): lax.psum_scatter(jnp.stack(partials), 'fsdp', scatter_dimension=1, tiled=...]
    all_gather x1 -> x0, waiting for transfers between devices: 119 us -> none  [shards(): lax.all_gather(compact, 'fsdp', axis=1, tiled=True)]
    pallas_call x0 -> x1, Pallas kernels: none -> 61.5 us  [shards(): pl.pallas_call(kernel, out_shape=(jax.ShapeDtypeStruct((1, 2, ROWS, 128),...]
    psum x1 -> x0, blocking collectives: 43.4 us -> none  [shards(): total = lax.psum(pseudo, 'rep')]
    dot_general x9 -> x0, matrix products: 20.1 us -> none  [the longest x2 6.49 us: layer_backward(): lax.dot_general(grad_pre, normed, (((0,), (0,)), ((), ())), preferred_ele...]
  transfers between devices with their start and end apart: 2 -> 0, of which waited for: 2 -> 0; matrix products, arithmetic and copies ran while one was open for 0% -> 0% of each run, Pallas kernels for 0% -> 0%
where the time goes in v1:
time: 67.3 us; the launch traced here: 67 us
  Pallas kernels  61.5 us (91%)
  local copies, waits for them, and re-layouts  4.16 us (6%)
  between operations  1.29 us (2%)
    pallas_call x1, Pallas kernels, shards(): pl.pallas_call(kernel, out_shape=(jax.ShapeDtypeStruct((1, 2, ROWS, 128),...  61.5 us
    unnamed x3, local copies, waits for them, and re-layouts  4.16 us

profile of v1, /device:TPU:1, one launch (start us, length us, event | category | flops | bytes accessed | tf_op | source)
XLA Modules:
  0.0 67.0 jit_solution(3862467301740385757)
XLA Ops:
  1.3 61.5 %window.1 = (f32[1,2,56,128]{3,2,1,0:T(8,128)}, f32[56,128]{1,0:T(8,128)}, f32[56,128]{1,0:T(8,128)}) custom-call(bf16[1,128,7168]{2,1,0:T(8,128)(2,1)} %x_h.1, bf16[1,128,7168]{2,1,0:T(8,128)(2,1)} %g_h.1, f32[1,2,56,128]{3,2,1,0:T(8,128)} %w_h.1, f32[1,2,56,128]{3,2,1,0:T(8,128)} %fm_h.1, f32[1,2,56,128]{3,2,1,0:T(8,128)} %sm_h.1, f32[56,128]{1,0:T(8,128)} %an_h.1, ...), custom_call_target="tpu_custom_call" | custom-call | tf_op jit(solution)/shard_map/window/pallas_call | solution.py:360
  62.8 1.4 %copy.15 = f32[1,2,56,128]{3,2,1,0:T(8,128)} copy(f32[1,2,56,128]{3,2,1,0:T(8,128)} %get-tuple-element.6) | data formatting | bytes 114688
  64.2 1.4 %copy.16 = f32[56,128]{1,0:T(8,128)} copy(f32[56,128]{1,0:T(8,128)} %get-tuple-element.7) | data formatting | bytes 57344
  65.6 1.4 %copy.17 = f32[56,128]{1,0:T(8,128)} copy(f32[56,128]{1,0:T(8,128)} %get-tuple-element.8) | data formatting | bytes 57344

commit v2 on v1

--- a/solution.py
+++ b/solution.py
@@ -40,11 +40,11 @@
 
 
 def kernel(
-    x_h, g_h, w_h, fm_h, sm_h, an_h, mo_h, fr,
+    x_h, g_h, w_h, fm_h, sm_h, an_h, mo_h, fr_h,
     new_w, new_a, new_m,
-    stack, w_all, send, recv, z_send, z_recv, w_own, fm, sm, an, mo, rep_send, rep_recv,
+    stack, across, w_all, send, recv, z_send, z_recv, w_own, fm, sm, an, mo, rep_send, rep_recv,
     proj, coef, expand, flat, ss,
-    load_sem, z_sems, ring_send, ring_recv, fwd_send, fwd_recv, tok_send, tok_recv,
+    step_s, load_sem, z_sems, ring_send, ring_recv, fwd_send, fwd_recv, tok_send, tok_recv,
     red_send, red_recv, rep_sems, rep_rsem,
 ):
     rep = lax.axis_index("rep")
@@ -101,6 +101,7 @@
                 (sm_h.at[0], sm),
                 (an_h, an),
                 (mo_h, mo),
+                (fr_h, step_s),
             ]
         )
     ]
@@ -110,9 +111,23 @@
     flat[pl.ds(0, ROWS, stride=2), :] = w_own[0]
     flat[pl.ds(1, ROWS, stride=2), :] = w_own[1]
     w_all[0, 0, place] = flat[...].astype(BF16).reshape(ROWS, 2, 128)
-    step = fr[0]
+    loads[7].wait()
+    step = step_s[0]
     chosen = lax.rem(step, 2).astype(F32)
     rep_send[...] = w_own[0] * (1.0 - chosen) + w_own[1] * chosen
+
+    def turn(start):
+        def one(r, _):
+            at = pl.multiple_of(r * 128, 128)
+            across[pl.ds(at, 128), start : start + TOK] = stack[pl.ds(start, TOK), pl.ds(at, 128)].T
+            return 0
+
+        lax.fori_loop(0, ROWS, one, 0, unroll=14)
+
+    loads[1].wait()
+    turn(0)
+    loads[2].wait()
+    turn(GRADS)
 
     pl.semaphore_wait(barrier, 1 + 1 + (PLANE - 1) + (REPS - 1))
 
@@ -146,22 +161,11 @@
     hand_on(0, place)
     tok_copies = []
     for i, start in enumerate((0, GRADS)):
-        loads[1 + i].wait()
         copy = remote(
             stack.at[pl.ds(start, TOK)], stack.at[pl.ds(start + TOK, TOK)], tok_send.at[i], tok_recv.at[i], sibling
         )
         copy.start()
         tok_copies.append(copy)
-    collect(0)
-    z_copy.wait_recv()
-    spread(1)
-    hand_on(1, place)
-
-    def rep_out(k, _):
-        remote(rep_send, rep_recv.at[rep], rep_sems, rep_rsem.at[rep], rep_peer(k)).start()
-        return 0
-
-    lax.fori_loop(1, REPS, rep_out, 0)
 
     def relayout(h):
         remote(w_all.at[h, 0], w_all.at[h, 1], fwd_send.at[h], fwd_recv.at[h], sibling).wait_recv()
@@ -172,32 +176,41 @@
                 stack[pl.ds(STACK + h * 64 + c * 32, 32), pl.ds(at, 128)] = w_all[h, c, :, r].reshape(32, 128)
             return 0
 
-        lax.fori_loop(0, ROWS, one, 0, unroll=4)
-
+        lax.fori_loop(0, ROWS, one, 0, unroll=8)
+
+    collect(0)
     relayout(0)
-    for copy in tok_copies:
+    z_copy.wait_recv()
+    spread(1)
+    hand_on(1, place)
+
+    def rep_out(k, _):
+        remote(rep_send, rep_recv.at[rep], rep_sems, rep_rsem.at[rep], rep_peer(k)).start()
+        return 0
+
+    lax.fori_loop(1, REPS, rep_out, 0)
+
+    for copy, start in zip(tok_copies, (TOK, GRADS + TOK), strict=True):
         copy.wait_recv()
+        turn(start)
 
     def square(r, acc):
-        v = stack[pl.ds(0, CHIP), pl.ds(pl.multiple_of(r * 128, 128), 128)].astype(F32)
-        return acc + v * v
-
-    acc = lax.fori_loop(0, ROWS, square, jnp.zeros((CHIP, 128), F32))
-    ss[...] = jnp.sum(acc.T, axis=0, keepdims=True)
+        v = across[pl.ds(pl.multiple_of(r * 128, 128), 128), 0:CHIP].astype(F32)
+        v = v * v
+        for i in range(16):
+            acc += v[i * 8 : i * 8 + 8]
+        return acc
+
+    acc = lax.fori_loop(0, ROWS, square, jnp.zeros((8, CHIP), F32), unroll=4)
+    ss[...] = jnp.sum(acc, axis=0, keepdims=True)
 
     collect(1)
     relayout(1)
 
-    proj[...] = jnp.zeros_like(proj)
-
-    def project(i, _):
-        at = pl.multiple_of(i * 1024, 1024)
-        out = dot(stack[pl.ds(STACK, 4 * H), pl.ds(at, 1024)], stack[:, pl.ds(at, 1024)], NT)
-        for j in range(ALL // 128):
-            proj[j] += out[:, j * 128 : (j + 1) * 128]
-        return 0
-
-    lax.fori_loop(0, D // 1024, project, 0)
+    with_tokens = dot(stack[STACK:ALL, :], across[...], NN)
+    for j in range(STACK // 128):
+        proj[j] = with_tokens[:, j * 128 : (j + 1) * 128]
+    proj[STACK // 128] = dot(stack[STACK:ALL, :], stack[STACK:ALL, :], NT)
 
     def rows_of(kind, layer, cols):
         return jnp.concatenate(
@@ -264,25 +277,24 @@
                     ]
 
     def gradients(h):
-        weights = jnp.concatenate([coef[j, pl.ds(h * 32, 32), :] for j in range(ALL // 128)], axis=1).astype(BF16)
-
-        def one(i, _):
-            at = pl.multiple_of(i * 512, 512)
-            out = dot(weights, stack[:, pl.ds(at, 512)], NN).astype(BF16)
-            for j in range(4):
-                send[h, :, i * 4 + j] = out[:, j * 128 : (j + 1) * 128].reshape(PLANE, 2, 128)
-            return 0
-
-        lax.fori_loop(0, D // 512, one, 0)
-
-        def out_one(k, _):
-            q = peer(k)
-            remote(
-                send.at[h, q], recv.at[h, place], red_send.at[h], red_recv.at[h], in_plane(q)
-            ).start()
-            return 0
-
-        lax.fori_loop(1, PLANE, out_one, 0)
+        weights = jnp.concatenate(
+            [coef[j, pl.ds(pl.multiple_of(h * 32, 32), 32), :] for j in range(ALL // 128)], axis=1
+        ).astype(BF16)
+        for part in range(2):
+            first = part * (ROWS // 2)
+            out = dot(weights, stack[:, first * 128 : (first + ROWS // 2) * 128], NN).astype(BF16)
+            for j in range(ROWS // 2):
+                send[h, :, first + j] = out[:, j * 128 : (j + 1) * 128].reshape(PLANE, 2, 128)
+            rows = pl.ds(first, ROWS // 2)
+
+            def out_one(k, _, rows=rows):
+                q = peer(k)
+                remote(
+                    send.at[h, q, rows], recv.at[h, place, rows], red_send.at[h], red_recv.at[h], in_plane(q)
+                ).start()
+                return 0
+
+            lax.fori_loop(1, PLANE, out_one, 0)
         recv[h, place] = send[h, place]
 
     def summed(h):
@@ -294,13 +306,13 @@
             total += recv[h, q].reshape(2 * ROWS, 128).astype(F32)
         return total
 
-    gradients(1)
-    gradients(0)
+    gradients(zh)
+    gradients(1 - zh)
     z_send[...] = summed(1).astype(BF16).reshape(ROWS, 2, 128)
     z_back = remote(z_send, z_recv, z_sems.at[2], z_sems.at[3], other_z)
     z_back.start()
 
-    for load in loads[3:]:
+    for load in loads[3:7]:
         load.wait()
 
     def rep_in(k, _):
@@ -352,22 +364,29 @@
     pltpu.make_async_copy(most, most, rep_sems).wait()
 
 
+def place_results(a, b, c, to_a, to_b, to_c):
+    to_a[...] = a[...]
+    to_b[...] = b[...]
+    to_c[...] = c[...]
+
+
 def shards(inputs, cotangent, weights, first_moment, second_moment, anchor, momentum, fragment):
-    any_space = pl.BlockSpec(memory_space=pl.ANY)
+    hbm = pl.BlockSpec(memory_space=pltpu.HBM)
     vmem = pl.BlockSpec(memory_space=pltpu.VMEM)
     dma = pltpu.SemaphoreType.DMA
     unit = (ROWS, 2, 128)
-    return pl.pallas_call(
+    results = pl.pallas_call(
         kernel,
         out_shape=(
-            jax.ShapeDtypeStruct((1, 2, ROWS, 128), F32),
-            jax.ShapeDtypeStruct((ROWS, 128), F32),
-            jax.ShapeDtypeStruct((ROWS, 128), F32),
+            pltpu.VMEM((1, 2, ROWS, 128), F32),
+            pltpu.VMEM((ROWS, 128), F32),
+            pltpu.VMEM((ROWS, 128), F32),
         ),
-        in_specs=[any_space] * 7 + [pl.BlockSpec(memory_space=pltpu.SMEM)],
+        in_specs=[hbm] * 8,
         out_specs=(vmem, vmem, vmem),
         scratch_shapes=[
             pltpu.VMEM((ALL, D), BF16),
+            pltpu.VMEM((D, STACK), BF16),
             pltpu.VMEM((2, 2, PLANE) + unit, BF16),
             pltpu.VMEM((2, PLANE) + unit, BF16),
             pltpu.VMEM((2, PLANE) + unit, BF16),
@@ -385,7 +404,8 @@
             pltpu.VMEM((2, 4 * H, 128), F32),
             pltpu.VMEM((2 * ROWS, 128), F32),
             pltpu.VMEM((1, CHIP), F32),
-            dma((7,)),
+            pltpu.SMEM((1,), jnp.int32),
+            dma((8,)),
             dma((4,)),
             dma((2,)),
             dma((2, PLANE)),
@@ -402,7 +422,19 @@
             collective_id=0, has_side_effects=True, vmem_limit_bytes=56 * 1024 * 1024
         ),
         name="window",
-    )(inputs, cotangent, weights, first_moment, second_moment, anchor, momentum, fragment)
+    )(
+        *(
+            a
+            for a in (inputs, cotangent, weights, first_moment, second_moment, anchor, momentum, fragment)
+        )
+    )
+    return pl.pallas_call(
+        place_results,
+        out_shape=tuple(jax.ShapeDtypeStruct(r.shape, r.dtype) for r in results),
+        in_specs=[vmem] * 3,
+        out_specs=(vmem,) * 3,
+        name="results",
+    )(*(pltpu.with_memory_space_constraint(r, pltpu.VMEM) for r in results))
 
 
 def solution(mesh):

time: 67.3 us -> 56.5 us (0.84)
  Pallas kernels: 61.5 us -> 55.1 us
  local copies, waits for them, and re-layouts: 4.16 us -> 0 us
    pallas_call x1 -> x2, Pallas kernels: 61.5 us -> 55.1 us  [the longest x1 54.4 us: shards(): pl.pallas_call(kernel, out_shape=(pltpu.VMEM((1, 2, ROWS, 128), F32), plt...]
    unnamed x3 -> x0, local copies, waits for them, and re-layouts: 4.16 us -> none
where the time goes in v2:
time: 56.5 us; the launch traced here: 56.4 us
  Pallas kernels  55.1 us (98%)
  between operations  1.29 us (2%)
    pallas_call x1, Pallas kernels, shards(): pl.pallas_call(kernel, out_shape=(pltpu.VMEM((1, 2, ROWS, 128), F32), plt...  54.4 us

profile of v2, /device:TPU:1, one launch (start us, length us, event | category | flops | bytes accessed | tf_op | source)
XLA Modules:
  0.0 56.4 jit_solution(4402271605816497919)
XLA Ops:
  1.3 54.4 %window.1 = (f32[1,2,56,128]{3,2,1,0:T(8,128)S(1)}, f32[56,128]{1,0:T(8,128)S(1)}, f32[56,128]{1,0:T(8,128)S(1)}) custom-call(bf16[1,128,7168]{2,1,0:T(8,128)(2,1)} %x_h.1, bf16[1,128,7168]{2,1,0:T(8,128)(2,1)} %g_h.1, f32[1,2,56,128]{3,2,1,0:T(8,128)} %w_h.1, f32[1,2,56,128]{3,2,1,0:T(8,128)} %fm_h.1, f32[1,2,56,128]{3,2,1,0:T(8,128)} %sm_h.1, ...), custom_call_target="tpu_custom_call" | custom-call | tf_op jit(solution)/shard_map/window/pallas_call | solution.py:378
  55.7 0.6 %results.1 = (f32[1,2,56,128]{3,2,1,0:T(8,128)}, f32[56,128]{1,0:T(8,128)}, f32[56,128]{1,0:T(8,128)}) custom-call(f32[1,2,56,128]{3,2,1,0:T(8,128)S(1)} %get-tuple-element.6.a, f32[56,128]{1,0:T(8,128)S(1)} %get-tuple-element.7.b, f32[56,128]{1,0:T(8,128)S(1)} %get-tuple-element.8.c), custom_call_target="tpu_custom_call" | custom-call | tf_op jit(solution)/shard_map/results/pallas_call | solution.py:431

commit v3 on v2

--- a/solution.py
+++ b/solution.py
@@ -42,10 +42,10 @@
 def kernel(
     x_h, g_h, w_h, fm_h, sm_h, an_h, mo_h, fr_h,
     new_w, new_a, new_m,
-    stack, across, w_all, send, recv, z_send, z_recv, w_own, fm, sm, an, mo, rep_send, rep_recv,
+    stack, across, w_all, send, recv, z_send, z_recv, staged, w_own, fm, sm, an, mo, rep_send, rep_recv,
     proj, coef, expand, flat, ss,
-    step_s, load_sem, z_sems, ring_send, ring_recv, fwd_send, fwd_recv, tok_send, tok_recv,
-    red_send, red_recv, rep_sems, rep_rsem,
+    step_s, load_sem, z_out, z_in, z_back_sems, ring_send, ring_recv, fwd_send, fwd_recv, tok_send, tok_recv,
+    red_send, red_recv, rep_out, rep_in, stage_out, stage_in, rest_out, there, ready,
 ):
     rep = lax.axis_index("rep")
     fsdp = lax.axis_index("fsdp")
@@ -59,11 +59,15 @@
     def in_plane(q):
         return (rep, q * 4 + zh * 2 + core)
 
+    early = zh == 0
+    late = zh == 1
     other_z = (rep, place * 4 + (1 - zh) * 2 + core)
     sibling = (rep, place * 4 + zh * 2 + (1 - core))
-
-    def rep_peer(k):
-        return (lax.rem(rep + k, REPS), fsdp)
+    across_rep = (
+        lax.rem(rep + 4, REPS),
+        rep + 2 - 4 * lax.rem(rep // 2, 2),
+        rep + 1 - 2 * lax.rem(rep, 2),
+    )
 
     def remote(src, dst, ssem, rsem, device):
         return pltpu.make_async_remote_copy(
@@ -75,17 +79,29 @@
     def greet(device):
         pl.semaphore_signal(barrier, inc=1, device_id=device, device_id_type=MESH)
 
-    greet(other_z)
-
-    def greet_rep(k, _):
-        greet(rep_peer(k))
-        return 0
-
-    lax.fori_loop(1, REPS, greet_rep, 0)
-    greet(sibling)
+    @pl.when(early & (core == 0))
+    def _():
+        greet((across_rep[0], fsdp))
+        greet((rep, fsdp + 2))
+        greet((across_rep[0], fsdp + 2))
+
+    @pl.when(early & (core == 1))
+    def _():
+        greet((rep, fsdp + 2))
+
+    @pl.when(late & (core == 1))
+    def _():
+        greet(sibling)
+
+    for r in across_rep:
+        greet((r, place * 4 + zh * 2 + 1))
+
+    @pl.when(core == 0)
+    def _():
+        greet(sibling)
 
     def greet_plane(k, _):
-        greet(in_plane(peer(k)))
+        greet((rep, peer(k) * 4 + zh * 2 + 1))
         return 0
 
     lax.fori_loop(1, PLANE, greet_plane, 0)
@@ -111,10 +127,19 @@
     flat[pl.ds(0, ROWS, stride=2), :] = w_own[0]
     flat[pl.ds(1, ROWS, stride=2), :] = w_own[1]
     w_all[0, 0, place] = flat[...].astype(BF16).reshape(ROWS, 2, 128)
+    z_copy = remote(w_all.at[0, 0, place], w_all.at[1, 0, place], z_out.at[0], z_in.at[0], other_z)
+
+    @pl.when(late & (core == 0))
+    def _():
+        pl.semaphore_wait(barrier, 3)
+        pl.semaphore_signal(there, inc=1, device_id=(across_rep[0], fsdp - 2), device_id_type=MESH)
+        z_copy.start()
+
     loads[7].wait()
     step = step_s[0]
     chosen = lax.rem(step, 2).astype(F32)
-    rep_send[...] = w_own[0] * (1.0 - chosen) + w_own[1] * chosen
+    loads[5].wait()
+    rep_send[0] = an[...] - (w_own[0] * (1.0 - chosen) + w_own[1] * chosen)
 
     def turn(start):
         def one(r, _):
@@ -129,10 +154,21 @@
     loads[2].wait()
     turn(GRADS)
 
-    pl.semaphore_wait(barrier, 1 + 1 + (PLANE - 1) + (REPS - 1))
-
-    z_copy = remote(w_all.at[0, 0, place], w_all.at[1, 0, place], z_sems.at[0], z_sems.at[1], other_z)
-    z_copy.start()
+    @pl.when(core == 1)
+    def _():
+        pl.semaphore_wait(barrier, 2 * PLANE - 1 + 2 * len(across_rep) + zh)
+        pl.semaphore_signal(ready, inc=1, device_id=sibling, device_id_type=MESH)
+
+    @pl.when(core == 0)
+    def _():
+        pl.semaphore_wait(ready, 1)
+
+    pair = remote(w_all.at[0, 0, place], w_all.at[0, 1, place], z_out.at[1], z_in.at[1], sibling)
+    pair.start()
+
+    @pl.when(late & (core == 1))
+    def _():
+        z_copy.start()
 
     def spread(h):
         def one(k, _):
@@ -158,7 +194,6 @@
         lax.fori_loop(1, PLANE, one, 0)
 
     spread(0)
-    hand_on(0, place)
     tok_copies = []
     for i, start in enumerate((0, GRADS)):
         copy = remote(
@@ -167,8 +202,50 @@
         copy.start()
         tok_copies.append(copy)
 
+    adds = [
+        remote(rep_send.at[i], rep_recv.at[i], rep_out.at[i], rep_in.at[i], (across_rep[i], fsdp)) for i in range(3)
+    ]
+    adds[0].start()
+
+    def hops():
+        half = [
+            remote(w_all.at[0, c, place], staged.at[c], stage_out.at[c], stage_in.at[c], (across_rep[0], fsdp))
+            for c in range(2)
+        ]
+        rest = [
+            remote(staged.at[c], w_all.at[1, 0, place], rest_out.at[c], z_in.at[0], (across_rep[0], fsdp + 2 + c))
+            for c in range(2)
+        ]
+        return half, rest
+
+    @pl.when(early & (core == 0))
+    def _():
+        half, rest = hops()
+        pl.semaphore_wait(barrier, 1)
+        pair.wait_recv()
+        for copy in half:
+            copy.start()
+        for copy in half:
+            copy.wait()
+        pl.semaphore_wait(there, 1)
+        for copy in rest:
+            copy.start()
+
+    @pl.when(late | (core == 1))
+    def _():
+        pair.wait_recv()
+
+    z_copy.wait_recv()
+    spread(1)
+    hand_on(1, place)
+
+    adds[0].wait_recv()
+    rep_send[1] = rep_send[0] + rep_recv[0]
+    adds[1].start()
+
     def relayout(h):
-        remote(w_all.at[h, 0], w_all.at[h, 1], fwd_send.at[h], fwd_recv.at[h], sibling).wait_recv()
+        most = w_all.at[h, 1, pl.ds(0, PLANE - 1 + h)]
+        remote(most, most, fwd_send.at[h], fwd_recv.at[h], sibling).wait_recv()
 
         def one(r, _):
             at = pl.multiple_of(r * 128, 128)
@@ -177,18 +254,6 @@
             return 0
 
         lax.fori_loop(0, ROWS, one, 0, unroll=8)
-
-    collect(0)
-    relayout(0)
-    z_copy.wait_recv()
-    spread(1)
-    hand_on(1, place)
-
-    def rep_out(k, _):
-        remote(rep_send, rep_recv.at[rep], rep_sems, rep_rsem.at[rep], rep_peer(k)).start()
-        return 0
-
-    lax.fori_loop(1, REPS, rep_out, 0)
 
     for copy, start in zip(tok_copies, (TOK, GRADS + TOK), strict=True):
         copy.wait_recv()
@@ -204,6 +269,11 @@
     acc = lax.fori_loop(0, ROWS, square, jnp.zeros((8, CHIP), F32), unroll=4)
     ss[...] = jnp.sum(acc, axis=0, keepdims=True)
 
+    collect(0)
+    relayout(0)
+    adds[1].wait_recv()
+    rep_send[2] = rep_send[1] + rep_recv[1]
+    adds[2].start()
     collect(1)
     relayout(1)
 
@@ -306,26 +376,17 @@
             total += recv[h, q].reshape(2 * ROWS, 128).astype(F32)
         return total
 
-    gradients(zh)
-    gradients(1 - zh)
+    gradients(1)
+    gradients(0)
     z_send[...] = summed(1).astype(BF16).reshape(ROWS, 2, 128)
-    z_back = remote(z_send, z_recv, z_sems.at[2], z_sems.at[3], other_z)
+    z_back = remote(z_send, z_recv, z_back_sems.at[0], z_back_sems.at[1], other_z)
     z_back.start()
 
-    for load in loads[3:7]:
+    for load in (loads[3], loads[4], loads[6]):
         load.wait()
-
-    def rep_in(k, _):
-        q = lax.rem(rep + k, REPS)
-        remote(rep_send, rep_recv.at[q], rep_sems, rep_rsem.at[q], rep_peer(k)).wait_recv()
-        return 0
-
-    lax.fori_loop(1, REPS, rep_in, 0)
-    rep_recv[rep] = rep_send[...]
+    adds[2].wait_recv()
+    total = rep_send[2] + rep_recv[2]
     anchor = an[...]
-    total = anchor - rep_recv[0]
-    for q in range(1, REPS):
-        total += anchor - rep_recv[q]
     delta = total * (1.0 / REPS)
     velocity = outer_beta * mo[...] + delta
     new_anchor = anchor - outer_rate * (delta + outer_beta * velocity)
@@ -350,18 +411,24 @@
         here = chosen if layer == 1 else 1.0 - chosen
         new_w[0, layer] = jnp.where(jnp.full((ROWS, 128), here, F32) > 0.5, merged, updated)
 
-    z_copy.wait_send()
-    z_back.wait_send()
-    for copy in tok_copies:
+    @pl.when(late)
+    def _():
+        z_copy.wait_send()
+
+    @pl.when(early & (core == 0))
+    def _():
+        for copy in hops()[1]:
+            copy.wait_send()
+
+    for copy in [pair, z_back, *tok_copies, *adds]:
         copy.wait_send()
     for h in range(2):
         most = w_all.at[h, 0, pl.ds(0, PLANE - 1)]
         pltpu.make_async_copy(most, most, ring_send.at[h]).wait()
-        pltpu.make_async_copy(w_all.at[h, 0], w_all.at[h, 0], fwd_send.at[h]).wait()
+        most = w_all.at[h, 0, pl.ds(0, PLANE - 1 + h)]
+        pltpu.make_async_copy(most, most, fwd_send.at[h]).wait()
         most = send.at[h, pl.ds(0, PLANE - 1)]
         pltpu.make_async_copy(most, most, red_send.at[h]).wait()
-    most = rep_recv.at[pl.ds(0, REPS - 1)]
-    pltpu.make_async_copy(most, most, rep_sems).wait()
 
 
 def place_results(a, b, c, to_a, to_b, to_c):
@@ -392,13 +459,14 @@
             pltpu.VMEM((2, PLANE) + unit, BF16),
             pltpu.VMEM(unit, BF16),
             pltpu.VMEM(unit, BF16),
+            pltpu.VMEM((2,) + unit, BF16),
             pltpu.VMEM((2, ROWS, 128), F32),
             pltpu.VMEM((2, ROWS, 128), F32),
             pltpu.VMEM((2, ROWS, 128), F32),
             pltpu.VMEM((ROWS, 128), F32),
             pltpu.VMEM((ROWS, 128), F32),
-            pltpu.VMEM((ROWS, 128), F32),
-            pltpu.VMEM((REPS, ROWS, 128), F32),
+            pltpu.VMEM((3, ROWS, 128), F32),
+            pltpu.VMEM((3, ROWS, 128), F32),
             pltpu.VMEM((ALL // 128, 4 * H, 128), F32),
             pltpu.VMEM((ALL // 128, 2 * H, 128), F32),
             pltpu.VMEM((2, 4 * H, 128), F32),
@@ -406,7 +474,9 @@
             pltpu.VMEM((1, CHIP), F32),
             pltpu.SMEM((1,), jnp.int32),
             dma((8,)),
-            dma((4,)),
+            dma((2,)),
+            dma((2,)),
+            dma((2,)),
             dma((2,)),
             dma((2, PLANE)),
             dma((2,)),
@@ -415,19 +485,19 @@
             dma((2,)),
             dma((2,)),
             dma((2,)),
-            dma,
-            dma((REPS,)),
+            dma((3,)),
+            dma((3,)),
+            dma((2,)),
+            dma((2,)),
+            dma((2,)),
+            pltpu.SemaphoreType.REGULAR,
+            pltpu.SemaphoreType.REGULAR,
         ],
         compiler_params=pltpu.CompilerParams(
             collective_id=0, has_side_effects=True, vmem_limit_bytes=56 * 1024 * 1024
         ),
         name="window",
-    )(
-        *(
-            a
-            for a in (inputs, cotangent, weights, first_moment, second_moment, anchor, momentum, fragment)
-        )
-    )
+    )(inputs, cotangent, weights, first_moment, second_moment, anchor, momentum, fragment)
     return pl.pallas_call(
         place_results,
         out_shape=tuple(jax.ShapeDtypeStruct(r.shape, r.dtype) for r in results),

time: 56.5 us -> 54.6 us (0.966)
  Pallas kernels: 55.1 us -> 52.8 us
    pallas_call x1, Pallas kernels: 54.4 us -> 52.2 us  [shards(): pl.pallas_call(kernel, out_shape=(pltpu.VMEM((1, 2, ROWS, 128), F32), plt...]
where the time goes in v3:
time: 54.6 us; the launch traced here: 54.1 us
  Pallas kernels  52.8 us (97%)
  between operations  1.29 us (2%)
    pallas_call x1, Pallas kernels, shards(): pl.pallas_call(kernel, out_shape=(pltpu.VMEM((1, 2, ROWS, 128), F32), plt...  52.2 us

profile of v3, /device:TPU:1, one launch (start us, length us, event | category | flops | bytes accessed | tf_op | source)
XLA Modules:
  0.0 54.1 jit_solution(5163789158781180650)
XLA Ops:
  1.3 52.2 %window.1 = (f32[1,2,56,128]{3,2,1,0:T(8,128)S(1)}, f32[56,128]{1,0:T(8,128)S(1)}, f32[56,128]{1,0:T(8,128)S(1)}) custom-call(bf16[1,128,7168]{2,1,0:T(8,128)(2,1)} %x_h.1, bf16[1,128,7168]{2,1,0:T(8,128)(2,1)} %g_h.1, f32[1,2,56,128]{3,2,1,0:T(8,128)} %w_h.1, f32[1,2,56,128]{3,2,1,0:T(8,128)} %fm_h.1, f32[1,2,56,128]{3,2,1,0:T(8,128)} %sm_h.1, ...), custom_call_target="tpu_custom_call" | custom-call | tf_op jit(solution)/shard_map/window/pallas_call | solution.py:445
  53.4 0.6 %results.1 = (f32[1,2,56,128]{3,2,1,0:T(8,128)}, f32[56,128]{1,0:T(8,128)}, f32[56,128]{1,0:T(8,128)}) custom-call(f32[1,2,56,128]{3,2,1,0:T(8,128)S(1)} %get-tuple-element.6.a, f32[56,128]{1,0:T(8,128)S(1)} %get-tuple-element.7.b, f32[56,128]{1,0:T(8,128)S(1)} %get-tuple-element.8.c), custom_call_target="tpu_custom_call" | custom-call | tf_op jit(solution)/shard_map/results/pallas_call | solution.py:501

commit v4 on v3

--- a/solution.py
+++ b/solution.py
@@ -44,8 +44,8 @@
     new_w, new_a, new_m,
     stack, across, w_all, send, recv, z_send, z_recv, staged, w_own, fm, sm, an, mo, rep_send, rep_recv,
     proj, coef, expand, flat, ss,
-    step_s, load_sem, z_out, z_in, z_back_sems, ring_send, ring_recv, fwd_send, fwd_recv, tok_send, tok_recv,
-    red_send, red_recv, rep_out, rep_in, stage_out, stage_in, rest_out, there, ready,
+    step_s, load_sem, z_sems, z_back_sems, ring_send, ring_recv, fwd_send, fwd_recv, tok_send, tok_recv,
+    red_send, red_recv, rep_out, rep_in, there, ready,
 ):
     rep = lax.axis_index("rep")
     fsdp = lax.axis_index("fsdp")
@@ -79,15 +79,21 @@
     def greet(device):
         pl.semaphore_signal(barrier, inc=1, device_id=device, device_id_type=MESH)
 
+    over = (rep, fsdp - core + 2 - 4 * zh)
+    over_staged = (across_rep[0], fsdp - core + 2 - 4 * zh)
+
     @pl.when(early & (core == 0))
     def _():
         greet((across_rep[0], fsdp))
+        greet(over)
+
+    @pl.when(early & (core == 1))
+    def _():
         greet((rep, fsdp + 2))
-        greet((across_rep[0], fsdp + 2))
-
-    @pl.when(early & (core == 1))
-    def _():
-        greet((rep, fsdp + 2))
+
+    @pl.when(early)
+    def _():
+        greet(over_staged)
 
     @pl.when(late & (core == 1))
     def _():
@@ -123,16 +129,28 @@
     ]
     for load in loads:
         load.start()
+    @pl.when(late & (core == 0))
+    def _():
+        pl.semaphore_wait(barrier, 4)
+        for c in range(2):
+            pl.semaphore_signal(there, inc=1, device_id=(across_rep[0], fsdp - 2 + c), device_id_type=MESH)
+
     loads[0].wait()
     flat[pl.ds(0, ROWS, stride=2), :] = w_own[0]
     flat[pl.ds(1, ROWS, stride=2), :] = w_own[1]
     w_all[0, 0, place] = flat[...].astype(BF16).reshape(ROWS, 2, 128)
-    z_copy = remote(w_all.at[0, 0, place], w_all.at[1, 0, place], z_out.at[0], z_in.at[0], other_z)
+    own = w_all.at[0, 0, place]
+    z_copy = remote(own, w_all.at[1, 0, place], z_sems.at[0], z_sems.at[1], other_z)
+    half = remote(own, staged, z_sems.at[2], z_sems.at[3], (across_rep[0], fsdp))
+    rest = remote(staged, w_all.at[1, 0, place], z_sems.at[0], z_sems.at[1], (across_rep[0], fsdp + 2 - 4 * zh))
+
+    @pl.when(early & (core == 0))
+    def _():
+        pl.semaphore_wait(barrier, 1)
+        half.start()
 
     @pl.when(late & (core == 0))
     def _():
-        pl.semaphore_wait(barrier, 3)
-        pl.semaphore_signal(there, inc=1, device_id=(across_rep[0], fsdp - 2), device_id_type=MESH)
         z_copy.start()
 
     loads[7].wait()
@@ -163,8 +181,9 @@
     def _():
         pl.semaphore_wait(ready, 1)
 
-    pair = remote(w_all.at[0, 0, place], w_all.at[0, 1, place], z_out.at[1], z_in.at[1], sibling)
-    pair.start()
+    @pl.when(early & (core == 1))
+    def _():
+        half.start()
 
     @pl.when(late & (core == 1))
     def _():
@@ -193,47 +212,28 @@
 
         lax.fori_loop(1, PLANE, one, 0)
 
+    @pl.when(early)
+    def _():
+        half.wait_recv()
+        pl.semaphore_wait(there, 1)
+        rest.start()
+
     spread(0)
+    hand_on(0, place)
     tok_copies = []
     for i, start in enumerate((0, GRADS)):
         copy = remote(
             stack.at[pl.ds(start, TOK)], stack.at[pl.ds(start + TOK, TOK)], tok_send.at[i], tok_recv.at[i], sibling
         )
-        copy.start()
         tok_copies.append(copy)
 
     adds = [
         remote(rep_send.at[i], rep_recv.at[i], rep_out.at[i], rep_in.at[i], (across_rep[i], fsdp)) for i in range(3)
     ]
+
+    for copy in tok_copies:
+        copy.start()
     adds[0].start()
-
-    def hops():
-        half = [
-            remote(w_all.at[0, c, place], staged.at[c], stage_out.at[c], stage_in.at[c], (across_rep[0], fsdp))
-            for c in range(2)
-        ]
-        rest = [
-            remote(staged.at[c], w_all.at[1, 0, place], rest_out.at[c], z_in.at[0], (across_rep[0], fsdp + 2 + c))
-            for c in range(2)
-        ]
-        return half, rest
-
-    @pl.when(early & (core == 0))
-    def _():
-        half, rest = hops()
-        pl.semaphore_wait(barrier, 1)
-        pair.wait_recv()
-        for copy in half:
-            copy.start()
-        for copy in half:
-            copy.wait()
-        pl.semaphore_wait(there, 1)
-        for copy in rest:
-            copy.start()
-
-    @pl.when(late | (core == 1))
-    def _():
-        pair.wait_recv()
 
     z_copy.wait_recv()
     spread(1)
@@ -244,7 +244,7 @@
     adds[1].start()
 
     def relayout(h):
-        most = w_all.at[h, 1, pl.ds(0, PLANE - 1 + h)]
+        most = w_all.at[h, 1]
         remote(most, most, fwd_send.at[h], fwd_recv.at[h], sibling).wait_recv()
 
         def one(r, _):
@@ -393,9 +393,9 @@
     new_m[...] = velocity
     new_a[...] = new_anchor
 
-    own = summed(0)
+    mine = summed(0)
     z_back.wait_recv()
-    flat[...] = (own + z_recv[...].reshape(2 * ROWS, 128).astype(F32)) * (1.0 / (TOK * 64))
+    flat[...] = (mine + z_recv[...].reshape(2 * ROWS, 128).astype(F32)) * (1.0 / (TOK * 64))
     count = jnp.full((8, 128), step.astype(F32), F32)
     correct_one = (1.0 - jnp.exp(count * math.log(beta_one)))[0:1]
     correct_two = (1.0 - jnp.exp(count * math.log(beta_two)))[0:1]
@@ -411,22 +411,17 @@
         here = chosen if layer == 1 else 1.0 - chosen
         new_w[0, layer] = jnp.where(jnp.full((ROWS, 128), here, F32) > 0.5, merged, updated)
 
-    @pl.when(late)
-    def _():
-        z_copy.wait_send()
-
-    @pl.when(early & (core == 0))
-    def _():
-        for copy in hops()[1]:
-            copy.wait_send()
-
-    for copy in [pair, z_back, *tok_copies, *adds]:
+    @pl.when(early)
+    def _():
+        half.wait_send()
+
+    z_copy.wait_send()
+    for copy in [z_back, *tok_copies, *adds]:
         copy.wait_send()
     for h in range(2):
         most = w_all.at[h, 0, pl.ds(0, PLANE - 1)]
         pltpu.make_async_copy(most, most, ring_send.at[h]).wait()
-        most = w_all.at[h, 0, pl.ds(0, PLANE - 1 + h)]
-        pltpu.make_async_copy(most, most, fwd_send.at[h]).wait()
+        pltpu.make_async_copy(w_all.at[h, 0], w_all.at[h, 0], fwd_send.at[h]).wait()
         most = send.at[h, pl.ds(0, PLANE - 1)]
         pltpu.make_async_copy(most, most, red_send.at[h]).wait()
 
@@ -459,7 +454,7 @@
             pltpu.VMEM((2, PLANE) + unit, BF16),
             pltpu.VMEM(unit, BF16),
             pltpu.VMEM(unit, BF16),
-            pltpu.VMEM((2,) + unit, BF16),
+            pltpu.VMEM(unit, BF16),
             pltpu.VMEM((2, ROWS, 128), F32),
             pltpu.VMEM((2, ROWS, 128), F32),
             pltpu.VMEM((2, ROWS, 128), F32),
@@ -474,8 +469,7 @@
             pltpu.VMEM((1, CHIP), F32),
             pltpu.SMEM((1,), jnp.int32),
             dma((8,)),
-            dma((2,)),
-            dma((2,)),
+            dma((4,)),
             dma((2,)),
             dma((2,)),
             dma((2, PLANE)),
@@ -487,9 +481,6 @@
             dma((2,)),
             dma((3,)),
             dma((3,)),
-            dma((2,)),
-            dma((2,)),
-            dma((2,)),
             pltpu.SemaphoreType.REGULAR,
             pltpu.SemaphoreType.REGULAR,
         ],

time: 54.6 us -> 52.4 us (0.960)
  Pallas kernels: 52.8 us -> 50.2 us
    pallas_call x1, Pallas kernels: 52.2 us -> 49.6 us  [shards(): pl.pallas_call(kernel, out_shape=(pltpu.VMEM((1, 2, ROWS, 128), F32), plt...]
where the time goes in v4:
time: 52.4 us; the launch traced here: 51.5 us
  Pallas kernels  50.2 us (96%)
  between operations  1.29 us (2%)
    pallas_call x1, Pallas kernels, shards(): pl.pallas_call(kernel, out_shape=(pltpu.VMEM((1, 2, ROWS, 128), F32), plt...  49.6 us

profile of v4, /device:TPU:1, one launch (start us, length us, event | category | flops | bytes accessed | tf_op | source)
XLA Modules:
  0.0 51.5 jit_solution(10774791845906399237)
XLA Ops:
  1.3 49.6 %window.1 = (f32[1,2,56,128]{3,2,1,0:T(8,128)S(1)}, f32[56,128]{1,0:T(8,128)S(1)}, f32[56,128]{1,0:T(8,128)S(1)}) custom-call(bf16[1,128,7168]{2,1,0:T(8,128)(2,1)} %x_h.1, bf16[1,128,7168]{2,1,0:T(8,128)(2,1)} %g_h.1, f32[1,2,56,128]{3,2,1,0:T(8,128)} %w_h.1, f32[1,2,56,128]{3,2,1,0:T(8,128)} %fm_h.1, f32[1,2,56,128]{3,2,1,0:T(8,128)} %sm_h.1, ...), custom_call_target="tpu_custom_call" | custom-call | tf_op jit(solution)/shard_map/window/pallas_call | solution.py:440
  50.9 0.6 %results.1 = (f32[1,2,56,128]{3,2,1,0:T(8,128)}, f32[56,128]{1,0:T(8,128)}, f32[56,128]{1,0:T(8,128)}) custom-call(f32[1,2,56,128]{3,2,1,0:T(8,128)S(1)} %get-tuple-element.6.a, f32[56,128]{1,0:T(8,128)S(1)} %get-tuple-element.7.b, f32[56,128]{1,0:T(8,128)S(1)} %get-tuple-element.8.c), custom_call_target="tpu_custom_call" | custom-call | tf_op jit(solution)/shard_map/results/pallas_call | solution.py:492

commit v5 on v4

--- a/solution.py
+++ b/solution.py
@@ -350,12 +350,12 @@
         weights = jnp.concatenate(
             [coef[j, pl.ds(pl.multiple_of(h * 32, 32), 32), :] for j in range(ALL // 128)], axis=1
         ).astype(BF16)
-        for part in range(2):
-            first = part * (ROWS // 2)
-            out = dot(weights, stack[:, first * 128 : (first + ROWS // 2) * 128], NN).astype(BF16)
-            for j in range(ROWS // 2):
+        for part in range(4):
+            first = part * (ROWS // 4)
+            out = dot(weights, stack[:, first * 128 : (first + ROWS // 4) * 128], NN).astype(BF16)
+            for j in range(ROWS // 4):
                 send[h, :, first + j] = out[:, j * 128 : (j + 1) * 128].reshape(PLANE, 2, 128)
-            rows = pl.ds(first, ROWS // 2)
+            rows = pl.ds(first, ROWS // 4)
 
             def out_one(k, _, rows=rows):
                 q = peer(k)
@@ -377,10 +377,19 @@
         return total
 
     gradients(1)
-    gradients(0)
+
+    @pl.when(early)
+    def _():
+        gradients(0)
+
     z_send[...] = summed(1).astype(BF16).reshape(ROWS, 2, 128)
     z_back = remote(z_send, z_recv, z_back_sems.at[0], z_back_sems.at[1], other_z)
     z_back.start()
+
+    @pl.when(late)
+    def _():
+        gradients(0)
+
 
     for load in (loads[3], loads[4], loads[6]):
         load.wait()

time: 52.4 us -> 51.4 us (0.981); the launches traced: 51.5 us -> 51.3 us
  no operation moved by 1% of the time
where the time goes in v5:
time: 51.4 us; the launch traced here: 51.3 us
  Pallas kernels  50 us (97%)
  between operations  1.29 us (3%)
    pallas_call x1, Pallas kernels, shards(): pl.pallas_call(kernel, out_shape=(pltpu.VMEM((1, 2, ROWS, 128), F32), plt...  49.3 us

profile of v5, /device:TPU:1, one launch (start us, length us, event | category | flops | bytes accessed | tf_op | source)
XLA Modules:
  0.0 51.3 jit_solution(9088465284531514901)
XLA Ops:
  1.3 49.3 %window.1 = (f32[1,2,56,128]{3,2,1,0:T(8,128)S(1)}, f32[56,128]{1,0:T(8,128)S(1)}, f32[56,128]{1,0:T(8,128)S(1)}) custom-call(bf16[1,128,7168]{2,1,0:T(8,128)(2,1)} %x_h.1, bf16[1,128,7168]{2,1,0:T(8,128)(2,1)} %g_h.1, f32[1,2,56,128]{3,2,1,0:T(8,128)} %w_h.1, f32[1,2,56,128]{3,2,1,0:T(8,128)} %fm_h.1, f32[1,2,56,128]{3,2,1,0:T(8,128)} %sm_h.1, ...), custom_call_target="tpu_custom_call" | custom-call | tf_op jit(solution)/shard_map/window/pallas_call | solution.py:449
  50.6 0.6 %results.1 = (f32[1,2,56,128]{3,2,1,0:T(8,128)}, f32[56,128]{1,0:T(8,128)}, f32[56,128]{1,0:T(8,128)}) custom-call(f32[1,2,56,128]{3,2,1,0:T(8,128)S(1)} %get-tuple-element.6.a, f32[56,128]{1,0:T(8,128)S(1)} %get-tuple-element.7.b, f32[56,128]{1,0:T(8,128)S(1)} %get-tuple-element.8.c), custom_call_target="tpu_custom_call" | custom-call | tf_op jit(solution)/shard_map/results/pallas_call | solution.py:501

commit v6 on v5

--- a/solution.py
+++ b/solution.py
@@ -357,23 +357,25 @@
                 send[h, :, first + j] = out[:, j * 128 : (j + 1) * 128].reshape(PLANE, 2, 128)
             rows = pl.ds(first, ROWS // 4)
 
-            def out_one(k, _, rows=rows):
+            def out_one(k, _, rows=rows, part=part):
                 q = peer(k)
                 remote(
-                    send.at[h, q, rows], recv.at[h, place, rows], red_send.at[h], red_recv.at[h], in_plane(q)
+                    send.at[h, q, rows], recv.at[h, place, rows], red_send.at[h], red_recv.at[h, part // 2], in_plane(q)
                 ).start()
                 return 0
 
             lax.fori_loop(1, PLANE, out_one, 0)
         recv[h, place] = send[h, place]
 
-    def summed(h):
-        pltpu.make_async_copy(
-            recv.at[h, pl.ds(0, PLANE - 1)], recv.at[h, pl.ds(0, PLANE - 1)], red_recv.at[h]
-        ).wait()
-        total = recv[h, 0].reshape(2 * ROWS, 128).astype(F32)
+    def rows_in(half):
+        return pl.ds(half * (ROWS // 2), ROWS // 2)
+
+    def summed(h, half):
+        most = recv.at[h, pl.ds(0, PLANE - 1), rows_in(half)]
+        pltpu.make_async_copy(most, most, red_recv.at[h, half]).wait()
+        total = recv[h, 0, rows_in(half)].reshape(ROWS, 128).astype(F32)
         for q in range(1, PLANE):
-            total += recv[h, q].reshape(2 * ROWS, 128).astype(F32)
+            total += recv[h, q, rows_in(half)].reshape(ROWS, 128).astype(F32)
         return total
 
     gradients(1)
@@ -382,9 +384,16 @@
     def _():
         gradients(0)
 
-    z_send[...] = summed(1).astype(BF16).reshape(ROWS, 2, 128)
-    z_back = remote(z_send, z_recv, z_back_sems.at[0], z_back_sems.at[1], other_z)
-    z_back.start()
+    z_backs = []
+    for half_at in range(2):
+        z_send[rows_in(half_at)] = summed(1, half_at).astype(BF16).reshape(ROWS // 2, 2, 128)
+        z_backs.append(
+            remote(
+                z_send.at[rows_in(half_at)], z_recv.at[rows_in(half_at)], z_back_sems.at[half_at],
+                z_back_sems.at[2 + half_at], other_z,
+            )
+        )
+        z_backs[half_at].start()
 
     @pl.when(late)
     def _():
@@ -402,12 +411,17 @@
     new_m[...] = velocity
     new_a[...] = new_anchor
 
-    mine = summed(0)
-    z_back.wait_recv()
-    flat[...] = (mine + z_recv[...].reshape(2 * ROWS, 128).astype(F32)) * (1.0 / (TOK * 64))
     count = jnp.full((8, 128), step.astype(F32), F32)
     correct_one = (1.0 - jnp.exp(count * math.log(beta_one)))[0:1]
     correct_two = (1.0 - jnp.exp(count * math.log(beta_two)))[0:1]
+    for half_at in range(2):
+        flat[pl.ds(half_at * ROWS, ROWS), :] = summed(0, half_at)
+    for half_at in range(2):
+        z_backs[half_at].wait_recv()
+        there_too = z_recv[rows_in(half_at)].reshape(ROWS, 128).astype(F32)
+        flat[pl.ds(half_at * ROWS, ROWS), :] = (flat[pl.ds(half_at * ROWS, ROWS), :] + there_too) * (
+            1.0 / (TOK * 64)
+        )
     for layer in range(2):
         gradient = flat[pl.ds(layer, ROWS, stride=2), :]
         params = w_own[layer]
@@ -425,7 +439,7 @@
         half.wait_send()
 
     z_copy.wait_send()
-    for copy in [z_back, *tok_copies, *adds]:
+    for copy in [*z_backs, *tok_copies, *adds]:
         copy.wait_send()
     for h in range(2):
         most = w_all.at[h, 0, pl.ds(0, PLANE - 1)]
@@ -479,7 +493,7 @@
             pltpu.SMEM((1,), jnp.int32),
             dma((8,)),
             dma((4,)),
-            dma((2,)),
+            dma((4,)),
             dma((2,)),
             dma((2, PLANE)),
             dma((2,)),
@@ -487,7 +501,7 @@
             dma((2,)),
             dma((2,)),
             dma((2,)),
-            dma((2,)),
+            dma((2, 2)),
             dma((3,)),
             dma((3,)),
             pltpu.SemaphoreType.REGULAR,

time: 51.4 us -> 51.1 us (level)
  no operation moved by 1% of the time
where the time goes in v6:
time: 51.1 us; the launch traced here: 51 us
  Pallas kernels  49.7 us (97%)
  between operations  1.29 us (3%)
    pallas_call x1, Pallas kernels, shards(): pl.pallas_call(kernel, out_shape=(pltpu.VMEM((1, 2, ROWS, 128), F32), plt...  49.1 us

profile of v6, /device:TPU:1, one launch (start us, length us, event | category | flops | bytes accessed | tf_op | source)
XLA Modules:
  0.0 51.0 jit_solution(2209195692051446144)
XLA Ops:
  1.3 49.1 %window.1 = (f32[1,2,56,128]{3,2,1,0:T(8,128)S(1)}, f32[56,128]{1,0:T(8,128)S(1)}, f32[56,128]{1,0:T(8,128)S(1)}) custom-call(bf16[1,128,7168]{2,1,0:T(8,128)(2,1)} %x_h.1, bf16[1,128,7168]{2,1,0:T(8,128)(2,1)} %g_h.1, f32[1,2,56,128]{3,2,1,0:T(8,128)} %w_h.1, f32[1,2,56,128]{3,2,1,0:T(8,128)} %fm_h.1, f32[1,2,56,128]{3,2,1,0:T(8,128)} %sm_h.1, ...), custom_call_target="tpu_custom_call" | custom-call | tf_op jit(solution)/shard_map/window/pallas_call | solution.py:463
  50.4 0.6 %results.1 = (f32[1,2,56,128]{3,2,1,0:T(8,128)}, f32[56,128]{1,0:T(8,128)}, f32[56,128]{1,0:T(8,128)}) custom-call(f32[1,2,56,128]{3,2,1,0:T(8,128)S(1)} %get-tuple-element.6.a, f32[56,128]{1,0:T(8,128)S(1)} %get-tuple-element.7.b, f32[56,128]{1,0:T(8,128)S(1)} %get-tuple-element.8.c), custom_call_target="tpu_custom_call" | custom-call | tf_op jit(solution)/shard_map/results/pallas_call | solution.py:515
